TPU v7x, 256 devices: a whole 4x4x8 slice. The times are simulated.
256 devices in a mesh: head: 4 (over x), inner: 4 (over y_hi, core), outer: 16 (over y_lo, z).
Axes of the slice: x: 4, y: 4 (y_hi: 2, y_lo: 2; y = y_hi * 2 + y_lo), z: 8, core: 2. Of those that a mesh axis runs over, the one named last changes fastest.
Arguments:
- saved_query: bfloat16 [8192, 2048], P(('outer', 'head', 'inner')), may hold values from -6 to 6
- saved_key: bfloat16 [8192, 2048], P(('outer', 'head', 'inner')), may hold values from -6 to 6
- saved_value: bfloat16 [8192, 2048], P(('outer', 'head', 'inner')), may hold values from -6 to 6
- saved_output: bfloat16 [8192, 2048], P(('outer', 'head', 'inner')), may hold values from -6 to 6
- output_grad: bfloat16 [8192, 2048], P(('outer', 'head', 'inner')), may hold values from -48 to 48
- saved_lse: float32 [16, 8192], P(('head', 'inner'), 'outer'), as said below
Outputs:
- query_grad: bfloat16 [8192, 2048], P(('outer', 'head', 'inner'))
- key_grad: bfloat16 [8192, 2048], P(('outer', 'head', 'inner'))
- value_grad: bfloat16 [8192, 2048], P(('outer', 'head', 'inner'))
Inputs may be any that keep to these rules, and one draw needn't show every extreme that they name: `saved_lse`: every entry lies between ln(8192) - 3 and ln(8192).
All inputs are finite; a program needn't handle non-finite values.
Results may differ from a plain program's by a relative error of at most 0.0062.
Values may be sent and summed in bfloat16 or wider, within the bound.
A program may use at most 64 MiB of HBM per device.

v0:
```python
import functools
import math

import jax
import jax.numpy as jnp
from jax import lax
from jax.experimental import pallas as pl
from jax.experimental.pallas import tpu as pltpu
from jax.sharding import PartitionSpec as P

HEAD_DIM = 128
SCALE = HEAD_DIM ** (-0.5)
LOG2E = math.log2(math.e)
MESH = pl.DeviceIdType.MESH


def packed(values, bits):
    per_word = 30 // bits
    words = [0] * ((len(values) + per_word - 1) // per_word)
    for place, value in enumerate(values):
        words[place // per_word] |= int(value) << (bits * (place % per_word))
    return words, per_word


def looked_up(table, bits, place):
    words, per_word = table
    found = words[0]
    for number in range(1, len(words)):
        found = jnp.where(place >= number * per_word, words[number], found)
    shift = lax.rem(place, per_word) * bits
    return lax.rem(lax.shift_right_logical(jnp.int32(found), shift), 1 << bits)


def dot_last(left, right):
    return lax.dot_general(left, right, (((1,), (1,)), ((), ())), preferred_element_type=jnp.float32)


def dot_first(left, right):
    return lax.dot_general(left, right, (((0,), (0,)), ((), ())), preferred_element_type=jnp.float32)


def dot_plain(left, right):
    return lax.dot_general(left, right, (((1,), (0,)), ((), ())), preferred_element_type=jnp.float32)


def offsets_near_first(count):
    order = [0]
    for step in range(1, count // 2 + 1):
        order.append(step)
        if count - step != step:
            order.append(count - step)
    return order


STEPS = (
    (0, 0, 0, 0),
    (0, 1, 0, 0),
    (0, 0, 1, 1),
    (1, 0, 0, 0),
    (1, 1, 0, 0),
    (1, 1, 1, 0),
    (1, 0, 1, 0),
    (0, 1, 1, 2),
    (0, 0, 1, 2),
)


def kernel(
    NX,
    NZ,
    q_ref,
    k_ref,
    v_ref,
    o_ref,
    g_ref,
    lse_ref,
    dq_out,
    dk_out,
    dv_out,
    lse_mem,
    q_mem,
    k_mem,
    v_mem,
    o_mem,
    g_mem,
    lse_send,
    lse_recv,
    del_send,
    del_recv,
    stats,
    qg,
    kv,
    kt,
    dq_acc,
    dkv_acc,
    dq_part,
    dq_recv,
    dkv_part,
    dkv_recv,
    fin,
    local_sem,
    s_lse,
    r_lse,
    s_del,
    r_del,
    s_in,
    r_in,
    s_stats,
    r_stats,
    s_qg,
    r_qg,
    s_kv,
    r_kv,
    s_dq,
    r_dq,
    s_dkv,
    r_dkv,
    s_out,
    r_out,
):
    half = q_ref.shape[1]
    peers = 2 * NZ
    wave_rows = peers * half
    home = 2 * wave_rows
    wave_lanes = wave_rows // 128
    per_row = 128 // half

    x = lax.axis_index("head")
    inner = lax.axis_index("inner")
    outer = lax.axis_index("outer")
    yh, c = inner // 2, lax.rem(inner, 2)
    yl, z = outer // NZ, lax.rem(outer, NZ)
    p = z * 2 + yh

    def device(dx, dyh, dyl, dz, dc):
        return {"head": dx, "inner": dyh * 2 + dc, "outer": dyl * NZ + dz}

    def head_of(dz, dyh):
        return (dz // 2) * 4 + (1 - dyh) * 2 + lax.rem(dz, 2)

    def ring_peer(step):
        turn = step // 2
        near = (turn + 1) // 2
        dz = lax.rem(jnp.where(lax.rem(turn, 2) == 1, z + near, z + NZ - near), NZ)
        return dz, lax.rem(yh + step, 2)

    def along_x(off):
        return device(lax.rem(x + off, NX), yh, yl, z, c)

    other_core = device(x, yh, yl, z, 1 - c)
    other_chip = device(x, yh, 1 - yl, z, c)

    lse_z, lse_yh = x * 2 + c, 1 - yh
    src_x, src_yh, src_c = z // 2, 1 - yh, lax.rem(z, 2)
    own_head = head_of(z, yh)

    barrier = pltpu.get_barrier_semaphore()

    def greet(where):
        pl.semaphore_signal(barrier, inc=1, device_id=where, device_id_type=MESH)

    ring = []
    for step in range(1, peers):
        dz, dyh = ring_peer(step)
        ring.append((dz * 2 + dyh, device(x, dyh, yl, dz, c), head_of(dz, dyh)))

    for _, where, _ in ring:
        greet(where)
    for off in range(1, NX):
        greet(along_x(off))
    greet(other_core)
    greet(other_chip)
    for dz in range(NZ):
        greet(device(src_x, src_yh, yl, dz, src_c))

    loads = [
        pltpu.make_async_copy(source, target, local_sem.at[number])
        for number, (source, target) in enumerate(
            (
                (lse_ref, lse_mem),
                (o_ref, o_mem),
                (g_ref, g_mem),
                (q_ref, q_mem),
                (k_ref, k_mem),
                (v_ref, v_mem),
            )
        )
    ]
    for load in loads:
        load.start()

    loads[0].wait()
    lane = lax.broadcasted_iota(jnp.int32, (8, 128), 1)
    for dx in range(NX):
        row = jnp.broadcast_to(lse_mem[:, dx * 128 : (dx + 1) * 128] * LOG2E, (8, 128))
        for dc in range(2):
            for wave in range(2):
                placed = jnp.zeros((8, 128), jnp.float32)
                for dyh in range(2):
                    spot = lax.rem(z * 2 + dyh, per_row) * half
                    turn = lax.rem(spot - (dyh * 64 + dc * 32 + wave * half) + 256, 128)
                    mine = (lane >= spot) & (lane < spot + half)
                    placed = jnp.where(mine, pltpu.roll(row, turn, 1), placed)
                lse_send[dx * 2 + dc, wave] = placed[:1]

    loads[1].wait()
    loads[2].wait()
    spot = lax.broadcasted_iota(jnp.int32, (half, 128), 0) + lax.rem(p, per_row) * half
    here = lax.broadcasted_iota(jnp.int32, (half, 128), 1) == spot
    for head in range(peers):
        cut = slice(head * HEAD_DIM, (head + 1) * HEAD_DIM)
        for wave in range(2):
            term = jnp.sum(
                o_mem[wave, :, cut].astype(jnp.float32) * g_mem[wave, :, cut].astype(jnp.float32),
                axis=1,
                keepdims=True,
            )
            del_send[head, wave] = jnp.sum(jnp.where(here, term, 0.0), axis=0, keepdims=True)
    del_recv[p] = del_send[own_head]

    pl.semaphore_wait(barrier, (peers - 1) + (NX - 1) + 2 + NX * 2)

    def columns(head):
        return pl.ds(pl.multiple_of(head * HEAD_DIM, HEAD_DIM), HEAD_DIM)

    def spot_of(which):
        return pl.ds(pl.multiple_of(which * half, half), half)

    def take(ref, sem):
        pltpu.make_async_copy(ref, ref, sem).wait()

    def push(source, target, send, recv, where):
        pltpu.make_async_remote_copy(
            src_ref=source,
            dst_ref=target,
            send_sem=send,
            recv_sem=recv,
            device_id=where,
            device_id_type=MESH,
        ).start()

    def send_rows(source, target, group):
        for _, where, head in ring:
            push(
                source.at[:, columns(head)],
                target.at[spot_of(p)],
                s_in.at[group],
                r_in.at[group],
                where,
            )
        pltpu.make_async_copy(
            source.at[:, columns(own_head)], target.at[spot_of(p)], r_in.at[group]
        ).start()

    def send_keys(number, wave):
        source = (k_mem, v_mem)[number]
        send_rows(source.at[wave], kv.at[number, yl, c, wave], 4 + number * 2 + wave)

    def send_queries(number, wave):
        source = (q_mem, g_mem)[number]
        send_rows(source.at[wave], qg.at[number, x, wave], number * 2 + wave)

    for dx in range(NX):
        for dc in range(2):
            push(
                lse_send.at[dx * 2 + dc],
                lse_recv.at[z],
                s_lse,
                r_lse,
                device(dx, lse_yh, yl, lse_z, dc),
            )
    for _, where, head in ring:
        push(del_send.at[head], del_recv.at[p], s_del, r_del, where)
    for load in loads[3:]:
        load.wait()
    for number, wave in ((0, 0), (1, 0)):
        send_queries(number, wave)
    for number, wave in ((0, 0), (1, 0), (0, 1)):
        send_keys(number, wave)
    send_queries(0, 1)
    send_keys(1, 1)
    send_queries(1, 1)

    dq_acc[...] = jnp.zeros_like(dq_acc)
    dkv_acc[...] = jnp.zeros_like(dkv_acc)

    def spread_keys(number, wave):
        block = kv.at[number, yl, c, wave]
        take(block, r_in.at[4 + number * 2 + wave])
        push(block, block, s_kv, r_kv.at[1, number, wave], other_chip)
        push(block, block, s_kv, r_kv.at[0, number, wave], other_core)

    def pass_keys(number, wave):
        block = kv.at[number, 1 - yl, c, wave]
        take(block, r_kv.at[1, number, wave])
        push(block, block, s_kv, r_kv.at[2, number, wave], other_core)

    def take_keys(way, block):
        for number in range(2):
            for wave in range(2):
                take(block.at[number, wave], r_kv.at[way, number, wave])

    def spread_queries(number, wave):
        block = qg.at[number, x, wave]
        take(block, r_in.at[number * 2 + wave])
        for off in near[1:]:
            push(block, block, s_qg, r_qg.at[off - 1, number, wave], along_x(off))

    def take_queries(wave):
        for off in near[1:]:
            for number in range(2):
                take(
                    qg.at[number, lax.rem(x - off + NX, NX), wave],
                    r_qg.at[off - 1, number, wave],
                )

    near = offsets_near_first(NX)
    take(lse_recv, r_lse)
    take(del_recv.at[pl.ds(0, peers - 1)], r_del)
    for wave in range(2):
        for row in range(wave_lanes):
            lse_row = jnp.zeros((1, 128), jnp.float32)
            for number in range(per_row // 2):
                lse_row = lse_row + lse_recv[row * (per_row // 2) + number, wave]
            stats[x, pl.ds(wave * wave_lanes + row, 1)] = lse_row
            del_row = jnp.zeros((1, 128), jnp.float32)
            for number in range(per_row):
                del_row = del_row + del_recv[row * per_row + number, wave]
            stats[x, pl.ds((2 + wave) * wave_lanes + row, 1)] = del_row
    for off in offsets_near_first(NX)[1:]:
        push(stats.at[x], stats.at[x], s_stats, r_stats.at[off - 1], along_x(off))
    spread_queries(0, 0)
    spread_queries(1, 0)
    spread_keys(0, 0)
    spread_keys(1, 0)
    spread_keys(0, 1)
    spread_queries(0, 1)
    spread_keys(1, 1)

    def send_back(which, wave, total):
        rows = pl.ds(wave * half, half)
        target = (dq_out, dk_out, dv_out)[which].at[rows, columns(own_head)]
        fin[which, wave] = total.astype(jnp.bfloat16).reshape(peers, half, HEAD_DIM)
        for index in range(peers):

            @pl.when(p != index)
            def _(index=index):
                push(
                    fin.at[which, wave, index],
                    target,
                    s_out.at[which, wave],
                    r_out.at[which, wave],
                    device(x, index % 2, yl, index // 2, c),
                )

        pltpu.make_async_copy(fin.at[which, wave, p], target, r_out.at[which, wave]).start()

    def finish_queries(wave):
        total = dq_acc[x, wave].T * SCALE
        for off in offsets_near_first(NX)[1:]:
            take(dq_recv.at[off - 1, wave], r_dq.at[off - 1, wave])
            total = total + dq_recv[off - 1, wave].astype(jnp.float32)
        send_back(0, wave, total)

    def key_part(which, side, core, wave):
        part = dkv_acc[which, side, core, pl.ds(wave * wave_rows, wave_rows)]
        return part * SCALE if which == 0 else part

    def send_core_part(slot, side):
        for which in range(2):
            for wave in range(2):
                part = key_part(which, side, 1 - c, wave)
                dkv_part[slot, which, wave] = part.astype(jnp.bfloat16)
            push(
                dkv_part.at[slot, which],
                dkv_recv.at[slot, which],
                s_dkv,
                r_dkv.at[slot, which, 0],
                other_core,
            )

    def turn_keys(side, yb, core):
        kt[side, core] = kv[0, yb, core].reshape(home, HEAD_DIM).T

    for off in near[1:]:
        take(stats.at[lax.rem(x - off + NX, NX)], r_stats.at[off - 1])
    turn_keys(0, yl, c)

    tables = [packed(column, 2) for column in zip(*STEPS)]

    def one_tile(side, core, off, wave):
        xb = lax.rem(x - off + NX, NX)
        yb = lax.rem(yl + side, 2)
        keys = kv[0, yb, core].reshape(home, HEAD_DIM)
        values = kv[1, yb, core].reshape(home, HEAD_DIM)
        queries, grads = qg[0, xb, wave], qg[1, xb, wave]

        def terms(kind):
            row = (kind * 2 + wave) * wave_lanes
            return jnp.concatenate(
                [stats[xb, pl.ds(row + number, 1)] for number in range(wave_lanes)], axis=1
            )

        scores = dot_last(keys, queries)
        dprobs = dot_last(values, grads)
        probs = jnp.exp2(scores * (SCALE * LOG2E) - terms(0))
        dscores = (probs * (dprobs - terms(1))).astype(jnp.bfloat16)
        dkv_acc[1, yb, core] += dot_plain(probs.astype(jnp.bfloat16), grads)
        dkv_acc[0, yb, core] += dot_plain(dscores, queries)
        dq_acc[xb, wave] += dot_plain(kt[side, core], dscores)

    def send_query_parts(wave):
        for off in near[1:]:
            xb = lax.rem(x - off + NX, NX)
            dq_part[off - 1, wave] = (dq_acc[xb, wave].T * SCALE).astype(jnp.bfloat16)
            push(
                dq_part.at[off - 1, wave],
                dq_recv.at[off - 1, wave],
                s_dq,
                r_dq.at[off - 1, wave],
                device(xb, yh, yl, z, c),
            )

    def step(number, carry):
        side, away, wave, kind = [looked_up(table, 2, number) for table in tables]
        core = lax.rem(c + away, 2)

        def at(place):
            return pl.when(number == place)

        @at(0)
        def _():
            take_queries(0)

        @at(1)
        def _():
            take_keys(0, kv.at[:, yl, 1 - c])
            turn_keys(0, yl, 1 - c)
            spread_queries(1, 1)
            pass_keys(0, 0)
            pass_keys(1, 0)

        @at(2)
        def _():
            pass_keys(0, 1)

        @at(3)
        def _():
            pass_keys(1, 1)
            turn_keys(1, 1 - yl, c)

        @at(4)
        def _():
            take_keys(2, kv.at[:, 1 - yl, 1 - c])
            turn_keys(1, 1 - yl, 1 - c)

        @at(5)
        def _():
            take_queries(1)

        @pl.when(kind == 0)
        def _():
            for off in near:
                one_tile(side, core, off, wave)

        @pl.when(kind == 1)
        def _():
            for other in range(2):
                one_tile(0, other, 0, 1)

        @pl.when(kind == 2)
        def _():
            for off in near[1:]:
                one_tile(0, core, off, 1)

        @at(4)
        def _():
            send_query_parts(0)

        @at(5)
        def _():
            send_core_part(0, 1 - yl)

        @at(6)
        def _():
            for which in range(2):
                take(dkv_recv.at[0, which], r_dkv.at[0, which, 0])
                for wave in range(2):
                    part = key_part(which, 1 - yl, c, wave)
                    part = part + dkv_recv[0, which, wave].astype(jnp.float32)
                    dkv_part[1, which, wave] = part.astype(jnp.bfloat16)
                    push(
                        dkv_part.at[1, which, wave],
                        dkv_recv.at[1, which, wave],
                        s_dkv,
                        r_dkv.at[1, which, wave],
                        other_chip,
                    )

        @at(7)
        def _():
            send_core_part(2, yl)
            finish_queries(0)

        @at(8)
        def _():
            send_query_parts(1)

        return carry

    lax.fori_loop(0, len(STEPS), step, 0)

    for which in range(2):
        take(dkv_recv.at[2, which], r_dkv.at[2, which, 0])
        for wave in range(2):
            total = key_part(which, yl, c, wave) + dkv_recv[2, which, wave].astype(jnp.float32)
            take(dkv_recv.at[1, which, wave], r_dkv.at[1, which, wave])
            send_back(1 + which, wave, total + dkv_recv[1, which, wave].astype(jnp.float32))
    finish_queries(1)

    take(lse_send, s_lse)
    take(del_send.at[pl.ds(0, peers - 1)], s_del)
    for wave in range(2):
        most = pl.ds(0, wave_rows - half)
        for number in range(2):
            take(kv.at[number, 0, 0, wave, most], s_in.at[4 + number * 2 + wave])
            take(qg.at[number, 0, wave, most], s_in.at[number * 2 + wave])
    take(stats.at[pl.ds(0, NX - 1)], s_stats)
    take(qg.at[:, pl.ds(0, NX - 1)], s_qg)
    take(kv.at[:, 0], s_kv)
    take(kv.at[:, 0, 0], s_kv)
    take(dq_part, s_dq)
    take(dkv_part, s_dkv)
    for which, target in ((0, dq_out), (1, dk_out), (2, dv_out)):
        for wave in range(2):
            take(fin.at[which, wave, pl.ds(0, peers - 1)], s_out.at[which, wave])
            take(target.at[pl.ds(wave * half, half)], r_out.at[which, wave])


def hand_over(dq_in, dk_in, dv_in, dq_out, dk_out, dv_out, held, in_sem, out_sem):
    loads = [
        pltpu.make_async_copy(source, held.at[number], in_sem.at[number])
        for number, source in enumerate((dq_in, dk_in, dv_in))
    ]
    stores = [
        pltpu.make_async_copy(held.at[number], target, out_sem.at[number])
        for number, target in enumerate((dq_out, dk_out, dv_out))
    ]
    for load in loads:
        load.start()
    for load, store in zip(loads, stores):
        load.wait()
        store.start()
    for store in stores:
        store.wait()


def solution(mesh):
    NX = mesh.shape["head"]
    NZ = mesh.shape["outer"] // 2

    def on_device(saved_query, saved_key, saved_value, saved_output, output_grad, saved_lse):
        rows, width = saved_query.shape
        half = rows // 2
        peers = 2 * NZ
        wave_rows = half * peers
        home = 2 * wave_rows
        bf16, f32 = jnp.bfloat16, jnp.float32
        anywhere = pl.BlockSpec(memory_space=pl.ANY)
        in_vmem = pl.BlockSpec(memory_space=pltpu.VMEM)
        lse_shape = saved_lse.shape
        result = jax.ShapeDtypeStruct((rows, width), bf16)
        dma = pltpu.SemaphoreType.DMA
        waves = [
            value.reshape(2, half, width)
            for value in (saved_query, saved_key, saved_value, saved_output, output_grad)
        ]
        grads = pl.pallas_call(
            functools.partial(kernel, NX, NZ),
            out_shape=(result, result, result),
            in_specs=[anywhere] * 6,
            out_specs=(anywhere, anywhere, anywhere),
            scratch_shapes=[
                pltpu.VMEM(lse_shape, f32),
                pltpu.VMEM((2, half, width), bf16),
                pltpu.VMEM((2, half, width), bf16),
                pltpu.VMEM((2, half, width), bf16),
                pltpu.VMEM((2, half, width), bf16),
                pltpu.VMEM((2, half, width), bf16),
                pltpu.VMEM((NX * 2, 2, 1, 128), f32),
                pltpu.VMEM((NZ, 2, 1, 128), f32),
                pltpu.VMEM((peers, 2, 1, 128), f32),
                pltpu.VMEM((peers, 2, 1, 128), f32),
                pltpu.VMEM((NX, 2 * home // 128, 128), f32),
                pltpu.VMEM((2, NX, 2, wave_rows, HEAD_DIM), bf16),
                pltpu.VMEM((2, 2, 2, 2, wave_rows, HEAD_DIM), bf16),
                pltpu.VMEM((2, 2, HEAD_DIM, home), bf16),
                pltpu.VMEM((NX, 2, HEAD_DIM, wave_rows), f32),
                pltpu.VMEM((2, 2, 2, home, HEAD_DIM), f32),
                pltpu.VMEM((NX - 1, 2, wave_rows, HEAD_DIM), bf16),
                pltpu.VMEM((NX - 1, 2, wave_rows, HEAD_DIM), bf16),
                pltpu.VMEM((3, 2, 2, wave_rows, HEAD_DIM), bf16),
                pltpu.VMEM((3, 2, 2, wave_rows, HEAD_DIM), bf16),
                pltpu.VMEM((3, 2, peers, half, HEAD_DIM), bf16),
                dma((6,)),
                dma,
                dma,
                dma,
                dma,
                dma((8,)),
                dma((8,)),
                dma,
                dma((NX - 1,)),
                dma,
                dma((NX - 1, 2, 2)),
                dma,
                dma((3, 2, 2)),
                dma,
                dma((NX - 1, 2)),
                dma,
                dma((3, 2, 2)),
                dma((3, 2)),
                dma((3, 2)),
            ],
            compiler_params=pltpu.CompilerParams(
                collective_id=0, has_side_effects=True, vmem_limit_bytes=60 * 2**20
            ),
            name="attention_backward",
        )(*waves, saved_lse)
        return pl.pallas_call(
            hand_over,
            out_shape=(result, result, result),
            in_specs=[anywhere] * 3,
            out_specs=(anywhere, anywhere, anywhere),
            scratch_shapes=[pltpu.VMEM((3, rows, width), bf16), dma((3,)), dma((3,))],
            compiler_params=pltpu.CompilerParams(vmem_limit_bytes=60 * 2**20),
            name="hand_over",
        )(*grads)

    rows_spec = P(("outer", "head", "inner"), None)
    return jax.shard_map(
        on_device,
        mesh=mesh,
        in_specs=(rows_spec,) * 5 + (P(("head", "inner"), "outer"),),
        out_specs=(rows_spec,) * 3,
        check_vma=False,
    )
```

profile of v0, /device:TPU:6, one launch (start us, length us, event | category | flops | bytes accessed | tf_op | source)
XLA Modules:
  0.0 57.9 jit_solution(455551105378083254)
XLA Ops:
  0.6 55.5 %attention_backward.1 = (bf16[32,2048]{1,0:T(8,128)(2,1)}, bf16[32,2048]{1,0:T(8,128)(2,1)}, bf16[32,2048]{1,0:T(8,128)(2,1)}) custom-call(bf16[2,16,2048]{2,1,0:T(8,128)(2,1)} %bitcast.5, bf16[2,16,2048]{2,1,0:T(8,128)(2,1)} %bitcast.6, bf16[2,16,2048]{2,1,0:T(8,128)(2,1)} %bitcast.7, bf16[2,16,2048]{2,1,0:T(8,128)(2,1)} %bitcast.8, ...), custom_call_target="tpu_custom_call" | custom-call | tf_op jit(solution)/shard_map/attention_backward/pallas_call | solution.py:578
  56.2 1.7 %hand_over.1 = (bf16[32,2048]{1,0:T(8,128)(2,1)}, bf16[32,2048]{1,0:T(8,128)(2,1)}, bf16[32,2048]{1,0:T(8,128)(2,1)}) custom-call(bf16[32,2048]{1,0:T(8,128)(2,1)} %get-tuple-element.6.dq_in, bf16[32,2048]{1,0:T(8,128)(2,1)} %get-tuple-element.7.dk_in, bf16[32,2048]{1,0:T(8,128)(2,1)} %get-tuple-element.8.dv_in), custom_call_target="tpu_custom_call" | custom-call | tf_op jit(solution)/shard_map/hand_over/pallas_call | solution.py:630
where the time goes:
time: 58 us; the launch traced here: 57.9 us
  Pallas kernels  57.3 us (99%)
  between operations  0.64 us (1%)
    pallas_call x1, Pallas kernels, on_device(): pl.pallas_call(functools.partial(kernel, NX, NZ), out_shape=(result, resu...  55.5 us
    pallas_call x1, Pallas kernels, on_device(): pl.pallas_call(hand_over, out_shape=(result, result, result), in_specs=[a...  1.74 us

commit v1 on v0

--- a/solution.py
+++ b/solution.py
@@ -77,6 +77,7 @@
     dq_out,
     dk_out,
     dv_out,
+    dv_other,
     lse_mem,
     q_mem,
     k_mem,
@@ -117,6 +118,8 @@
     r_dkv,
     s_out,
     r_out,
+    s_far,
+    r_far,
 ):
     half = q_ref.shape[1]
     peers = 2 * NZ
@@ -169,7 +172,8 @@
     for off in range(1, NX):
         greet(along_x(off))
     greet(other_core)
-    greet(other_chip)
+    for index in range(peers):
+        greet(device(x, index % 2, 1 - yl, index // 2, c))
     for dz in range(NZ):
         greet(device(src_x, src_yh, yl, dz, src_c))
 
@@ -218,7 +222,7 @@
             del_send[head, wave] = jnp.sum(jnp.where(here, term, 0.0), axis=0, keepdims=True)
     del_recv[p] = del_send[own_head]
 
-    pl.semaphore_wait(barrier, (peers - 1) + (NX - 1) + 2 + NX * 2)
+    pl.semaphore_wait(barrier, (peers - 1) + (NX - 1) + 1 + peers + NX * 2)
 
     def columns(head):
         return pl.ds(pl.multiple_of(head * HEAD_DIM, HEAD_DIM), HEAD_DIM)
@@ -489,13 +493,23 @@
                     part = key_part(which, 1 - yl, c, wave)
                     part = part + dkv_recv[0, which, wave].astype(jnp.float32)
                     dkv_part[1, which, wave] = part.astype(jnp.bfloat16)
-                    push(
-                        dkv_part.at[1, which, wave],
-                        dkv_recv.at[1, which, wave],
-                        s_dkv,
-                        r_dkv.at[1, which, wave],
-                        other_chip,
-                    )
+                    if which == 0 or wave == 0:
+                        push(
+                            dkv_part.at[1, which, wave],
+                            dkv_recv.at[1, which, wave],
+                            s_dkv,
+                            r_dkv.at[1, which, wave],
+                            other_chip,
+                        )
+                        continue
+                    for index in range(peers):
+                        push(
+                            dkv_part.at[1, which, wave, pl.ds(index * half, half)],
+                            dv_other.at[:, columns(own_head)],
+                            s_far,
+                            r_far,
+                            device(x, index % 2, 1 - yl, index // 2, c),
+                        )
 
         @at(7)
         def _():
@@ -512,10 +526,13 @@
 
     for which in range(2):
         take(dkv_recv.at[2, which], r_dkv.at[2, which, 0])
-        for wave in range(2):
+    for which, wave in ((1, 1), (0, 0), (0, 1), (1, 0)):
+        if True:
             total = key_part(which, yl, c, wave) + dkv_recv[2, which, wave].astype(jnp.float32)
-            take(dkv_recv.at[1, which, wave], r_dkv.at[1, which, wave])
-            send_back(1 + which, wave, total + dkv_recv[1, which, wave].astype(jnp.float32))
+            if which == 0 or wave == 0:
+                take(dkv_recv.at[1, which, wave], r_dkv.at[1, which, wave])
+                total = total + dkv_recv[1, which, wave].astype(jnp.float32)
+            send_back(1 + which, wave, total)
     finish_queries(1)
 
     take(lse_send, s_lse)
@@ -530,27 +547,40 @@
     take(kv.at[:, 0], s_kv)
     take(kv.at[:, 0, 0], s_kv)
     take(dq_part, s_dq)
-    take(dkv_part, s_dkv)
+    take(dkv_part.at[0], s_dkv)
+    take(dkv_part.at[1, 0], s_dkv)
+    take(dkv_part.at[2], s_dkv)
+    take(dkv_part.at[1, 1, 0], s_dkv)
+    take(dkv_part.at[1, 1, 1], s_far)
+    take(dv_other, r_far)
     for which, target in ((0, dq_out), (1, dk_out), (2, dv_out)):
         for wave in range(2):
             take(fin.at[which, wave, pl.ds(0, peers - 1)], s_out.at[which, wave])
             take(target.at[pl.ds(wave * half, half)], r_out.at[which, wave])
 
 
-def hand_over(dq_in, dk_in, dv_in, dq_out, dk_out, dv_out, held, in_sem, out_sem):
+def hand_over(dq_in, dk_in, dv_in, dv_more, dq_out, dk_out, dv_out, held, more, in_sem, out_sem):
     loads = [
         pltpu.make_async_copy(source, held.at[number], in_sem.at[number])
-        for number, source in enumerate((dq_in, dk_in, dv_in))
+        for number, source in enumerate((dv_in, dq_in, dk_in))
     ]
     stores = [
         pltpu.make_async_copy(held.at[number], target, out_sem.at[number])
-        for number, target in enumerate((dq_out, dk_out, dv_out))
+        for number, target in enumerate((dv_out, dq_out, dk_out))
     ]
+    loads.append(pltpu.make_async_copy(dv_more, more, in_sem.at[3]))
     for load in loads:
         load.start()
-    for load, store in zip(loads, stores):
-        load.wait()
-        store.start()
+    loads[1].wait()
+    stores[1].start()
+    loads[2].wait()
+    stores[2].start()
+    loads[0].wait()
+    loads[3].wait()
+    half = more.shape[0]
+    total = held[0, half:].astype(jnp.float32) + more[...].astype(jnp.float32)
+    held[0, half:] = total.astype(jnp.bfloat16)
+    stores[0].start()
     for store in stores:
         store.wait()
 
@@ -577,9 +607,9 @@
         ]
         grads = pl.pallas_call(
             functools.partial(kernel, NX, NZ),
-            out_shape=(result, result, result),
+            out_shape=(result,) * 3 + (jax.ShapeDtypeStruct((half, width), bf16),),
             in_specs=[anywhere] * 6,
-            out_specs=(anywhere, anywhere, anywhere),
+            out_specs=(anywhere,) * 4,
             scratch_shapes=[
                 pltpu.VMEM(lse_shape, f32),
                 pltpu.VMEM((2, half, width), bf16),
@@ -621,6 +651,8 @@
                 dma((3, 2, 2)),
                 dma((3, 2)),
                 dma((3, 2)),
+                dma,
+                dma,
             ],
             compiler_params=pltpu.CompilerParams(
                 collective_id=0, has_side_effects=True, vmem_limit_bytes=60 * 2**20
@@ -630,9 +662,14 @@
         return pl.pallas_call(
             hand_over,
             out_shape=(result, result, result),
-            in_specs=[anywhere] * 3,
+            in_specs=[anywhere] * 4,
             out_specs=(anywhere, anywhere, anywhere),
-            scratch_shapes=[pltpu.VMEM((3, rows, width), bf16), dma((3,)), dma((3,))],
+            scratch_shapes=[
+                pltpu.VMEM((3, rows, width), bf16),
+                pltpu.VMEM((half, width), bf16),
+                dma((4,)),
+                dma((3,)),
+            ],
             compiler_params=pltpu.CompilerParams(vmem_limit_bytes=60 * 2**20),
             name="hand_over",
         )(*grads)

time: 58 us -> 57.3 us (0.988)
  Pallas kernels: 57.3 us -> 56.6 us
    pallas_call x1, Pallas kernels: 55.5 us -> 54.8 us  [on_device(): pl.pallas_call(functools.partial(kernel, NX, NZ), out_shape=(result,) * 3...]
where the time goes in v1:
time: 57.3 us; the launch traced here: 57.2 us
  Pallas kernels  56.6 us (99%)
  between operations  0.64 us (1%)
    pallas_call x1, Pallas kernels, on_device(): pl.pallas_call(functools.partial(kernel, NX, NZ), out_shape=(result,) * 3...  54.8 us
    pallas_call x1, Pallas kernels, on_device(): pl.pallas_call(hand_over, out_shape=(result, result, result), in_specs=[a...  1.79 us

profile of v1, /device:TPU:6, one launch (start us, length us, event | category | flops | bytes accessed | tf_op | source)
XLA Modules:
  0.0 57.2 jit_solution(13687501968875382432)
XLA Ops:
  0.6 54.8 %attention_backward.1 = (bf16[32,2048]{1,0:T(8,128)(2,1)}, bf16[32,2048]{1,0:T(8,128)(2,1)}, bf16[32,2048]{1,0:T(8,128)(2,1)}, bf16[16,2048]{1,0:T(8,128)(2,1)}) custom-call(bf16[2,16,2048]{2,1,0:T(8,128)(2,1)} %bitcast.5, bf16[2,16,2048]{2,1,0:T(8,128)(2,1)} %bitcast.6, bf16[2,16,2048]{2,1,0:T(8,128)(2,1)} %bitcast.7, bf16[2,16,2048]{2,1,0:T(8,128)(2,1)} %bitcast.8, ...), custom_call_target="tpu_custom_call" | custom-call | tf_op jit(solution)/shard_map/attention_backward/pallas_call | solution.py:608
  55.4 1.8 %hand_over.1 = (bf16[32,2048]{1,0:T(8,128)(2,1)}, bf16[32,2048]{1,0:T(8,128)(2,1)}, bf16[32,2048]{1,0:T(8,128)(2,1)}) custom-call(bf16[32,2048]{1,0:T(8,128)(2,1)} %get-tuple-element.7.dq_in, bf16[32,2048]{1,0:T(8,128)(2,1)} %get-tuple-element.8.dk_in, bf16[32,2048]{1,0:T(8,128)(2,1)} %get-tuple-element.9.dv_in, bf16[16,2048]{1,0:T(8,128)(2,1)} %get-tuple-element.10.dv_more), custom_call_target="tpu_custom_call" | custom-call | tf_op jit(solution)/shard_map/hand_over/pallas_call | solution.py:662

commit v2 on v1

--- a/solution.py
+++ b/solution.py
@@ -12,23 +12,6 @@
 SCALE = HEAD_DIM ** (-0.5)
 LOG2E = math.log2(math.e)
 MESH = pl.DeviceIdType.MESH
-
-
-def packed(values, bits):
-    per_word = 30 // bits
-    words = [0] * ((len(values) + per_word - 1) // per_word)
-    for place, value in enumerate(values):
-        words[place // per_word] |= int(value) << (bits * (place % per_word))
-    return words, per_word
-
-
-def looked_up(table, bits, place):
-    words, per_word = table
-    found = words[0]
-    for number in range(1, len(words)):
-        found = jnp.where(place >= number * per_word, words[number], found)
-    shift = lax.rem(place, per_word) * bits
-    return lax.rem(lax.shift_right_logical(jnp.int32(found), shift), 1 << bits)
 
 
 def dot_last(left, right):
@@ -167,15 +150,14 @@
         dz, dyh = ring_peer(step)
         ring.append((dz * 2 + dyh, device(x, dyh, yl, dz, c), head_of(dz, dyh)))
 
+    for dz in range(NZ):
+        greet(device(src_x, src_yh, yl, dz, src_c))
     for _, where, _ in ring:
         greet(where)
     for off in range(1, NX):
         greet(along_x(off))
     greet(other_core)
-    for index in range(peers):
-        greet(device(x, index % 2, 1 - yl, index // 2, c))
-    for dz in range(NZ):
-        greet(device(src_x, src_yh, yl, dz, src_c))
+    greet(other_chip)
 
     loads = [
         pltpu.make_async_copy(source, target, local_sem.at[number])
@@ -222,7 +204,7 @@
             del_send[head, wave] = jnp.sum(jnp.where(here, term, 0.0), axis=0, keepdims=True)
     del_recv[p] = del_send[own_head]
 
-    pl.semaphore_wait(barrier, (peers - 1) + (NX - 1) + 1 + peers + NX * 2)
+    pl.semaphore_wait(barrier, (peers - 1) + (NX - 1) + 2 + NX * 2)
 
     def columns(head):
         return pl.ds(pl.multiple_of(head * HEAD_DIM, HEAD_DIM), HEAD_DIM)
@@ -390,8 +372,6 @@
         take(stats.at[lax.rem(x - off + NX, NX)], r_stats.at[off - 1])
     turn_keys(0, yl, c)
 
-    tables = [packed(column, 2) for column in zip(*STEPS)]
-
     def one_tile(side, core, off, wave):
         xb = lax.rem(x - off + NX, NX)
         yb = lax.rem(yl + side, 2)
@@ -425,12 +405,15 @@
                 device(xb, yh, yl, z, c),
             )
 
-    def step(number, carry):
-        side, away, wave, kind = [looked_up(table, 2, number) for table in tables]
+    def step(number):
+        side, away, wave, kind = STEPS[number]
         core = lax.rem(c + away, 2)
 
         def at(place):
-            return pl.when(number == place)
+            return lambda body: body() if number == place else None
+
+        def of_kind(which):
+            return lambda body: body() if kind == which else None
 
         @at(0)
         def _():
@@ -462,17 +445,17 @@
         def _():
             take_queries(1)
 
-        @pl.when(kind == 0)
+        @of_kind(0)
         def _():
             for off in near:
                 one_tile(side, core, off, wave)
 
-        @pl.when(kind == 1)
+        @of_kind(1)
         def _():
             for other in range(2):
                 one_tile(0, other, 0, 1)
 
-        @pl.when(kind == 2)
+        @of_kind(2)
         def _():
             for off in near[1:]:
                 one_tile(0, core, off, 1)
@@ -520,9 +503,8 @@
         def _():
             send_query_parts(1)
 
-        return carry
-
-    lax.fori_loop(0, len(STEPS), step, 0)
+    for number in range(len(STEPS)):
+        step(number)
 
     for which in range(2):
         take(dkv_recv.at[2, which], r_dkv.at[2, which, 0])

time: 57.3 us -> 56.4 us (0.984)
  Pallas kernels: 56.6 us -> 55.7 us
    pallas_call x1, Pallas kernels: 54.8 us -> 53.9 us  [on_device(): pl.pallas_call(functools.partial(kernel, NX, NZ), out_shape=(result,) * 3...]
where the time goes in v2:
time: 56.4 us; the launch traced here: 56.3 us
  Pallas kernels  55.7 us (99%)
  between operations  0.64 us (1%)
    pallas_call x1, Pallas kernels, on_device(): pl.pallas_call(functools.partial(kernel, NX, NZ), out_shape=(result,) * 3...  53.9 us
    pallas_call x1, Pallas kernels, on_device(): pl.pallas_call(hand_over, out_shape=(result, result, result), in_specs=[a...  1.79 us

profile of v2, /device:TPU:6, one launch (start us, length us, event | category | flops | bytes accessed | tf_op | source)
XLA Modules:
  0.0 56.3 jit_solution(8102971395530804620)
XLA Ops:
  0.6 53.9 %attention_backward.1 = (bf16[32,2048]{1,0:T(8,128)(2,1)}, bf16[32,2048]{1,0:T(8,128)(2,1)}, bf16[32,2048]{1,0:T(8,128)(2,1)}, bf16[16,2048]{1,0:T(8,128)(2,1)}) custom-call(bf16[2,16,2048]{2,1,0:T(8,128)(2,1)} %bitcast.5, bf16[2,16,2048]{2,1,0:T(8,128)(2,1)} %bitcast.6, bf16[2,16,2048]{2,1,0:T(8,128)(2,1)} %bitcast.7, bf16[2,16,2048]{2,1,0:T(8,128)(2,1)} %bitcast.8, ...), custom_call_target="tpu_custom_call" | custom-call | tf_op jit(solution)/shard_map/attention_backward/pallas_call | solution.py:590
  54.5 1.8 %hand_over.1 = (bf16[32,2048]{1,0:T(8,128)(2,1)}, bf16[32,2048]{1,0:T(8,128)(2,1)}, bf16[32,2048]{1,0:T(8,128)(2,1)}) custom-call(bf16[32,2048]{1,0:T(8,128)(2,1)} %get-tuple-element.7.dq_in, bf16[32,2048]{1,0:T(8,128)(2,1)} %get-tuple-element.8.dk_in, bf16[32,2048]{1,0:T(8,128)(2,1)} %get-tuple-element.9.dv_in, bf16[16,2048]{1,0:T(8,128)(2,1)} %get-tuple-element.10.dv_more), custom_call_target="tpu_custom_call" | custom-call | tf_op jit(solution)/shard_map/hand_over/pallas_call | solution.py:644

commit v3 on v2

--- a/solution.py
+++ b/solution.py
@@ -497,11 +497,11 @@
         @at(7)
         def _():
             send_core_part(2, yl)
+
+        @at(8)
+        def _():
+            send_query_parts(1)
             finish_queries(0)
-
-        @at(8)
-        def _():
-            send_query_parts(1)
 
     for number in range(len(STEPS)):
         step(number)
@@ -509,14 +509,14 @@
     for which in range(2):
         take(dkv_recv.at[2, which], r_dkv.at[2, which, 0])
     for which, wave in ((1, 1), (0, 0), (0, 1), (1, 0)):
+        if (which, wave) == (1, 0):
+            finish_queries(1)
         if True:
             total = key_part(which, yl, c, wave) + dkv_recv[2, which, wave].astype(jnp.float32)
             if which == 0 or wave == 0:
                 take(dkv_recv.at[1, which, wave], r_dkv.at[1, which, wave])
                 total = total + dkv_recv[1, which, wave].astype(jnp.float32)
             send_back(1 + which, wave, total)
-    finish_queries(1)
-
     take(lse_send, s_lse)
     take(del_send.at[pl.ds(0, peers - 1)], s_del)
     for wave in range(2):

time: 56.4 us -> 56 us (level)
  Pallas kernels: 55.7 us -> 55.1 us
    pallas_call x1, Pallas kernels: 53.9 us -> 53.3 us  [on_device(): pl.pallas_call(functools.partial(kernel, NX, NZ), out_shape=(result,) * 3...]
where the time goes in v3:
time: 56 us; the launch traced here: 55.7 us
  Pallas kernels  55.1 us (98%)
  between operations  0.64 us (1%)
    pallas_call x1, Pallas kernels, on_device(): pl.pallas_call(functools.partial(kernel, NX, NZ), out_shape=(result,) * 3...  53.3 us
    pallas_call x1, Pallas kernels, on_device(): pl.pallas_call(hand_over, out_shape=(result, result, result), in_specs=[a...  1.79 us

profile of v3, /device:TPU:6, one launch (start us, length us, event | category | flops | bytes accessed | tf_op | source)
XLA Modules:
  0.0 55.7 jit_solution(15700314336162567275)
XLA Ops:
  0.6 53.3 %attention_backward.1 = (bf16[32,2048]{1,0:T(8,128)(2,1)}, bf16[32,2048]{1,0:T(8,128)(2,1)}, bf16[32,2048]{1,0:T(8,128)(2,1)}, bf16[16,2048]{1,0:T(8,128)(2,1)}) custom-call(bf16[2,16,2048]{2,1,0:T(8,128)(2,1)} %bitcast.5, bf16[2,16,2048]{2,1,0:T(8,128)(2,1)} %bitcast.6, bf16[2,16,2048]{2,1,0:T(8,128)(2,1)} %bitcast.7, bf16[2,16,2048]{2,1,0:T(8,128)(2,1)} %bitcast.8, ...), custom_call_target="tpu_custom_call" | custom-call | tf_op jit(solution)/shard_map/attention_backward/pallas_call | solution.py:590
  53.9 1.8 %hand_over.1 = (bf16[32,2048]{1,0:T(8,128)(2,1)}, bf16[32,2048]{1,0:T(8,128)(2,1)}, bf16[32,2048]{1,0:T(8,128)(2,1)}) custom-call(bf16[32,2048]{1,0:T(8,128)(2,1)} %get-tuple-element.7.dq_in, bf16[32,2048]{1,0:T(8,128)(2,1)} %get-tuple-element.8.dk_in, bf16[32,2048]{1,0:T(8,128)(2,1)} %get-tuple-element.9.dv_in, bf16[16,2048]{1,0:T(8,128)(2,1)} %get-tuple-element.10.dv_more), custom_call_target="tpu_custom_call" | custom-call | tf_op jit(solution)/shard_map/hand_over/pallas_call | solution.py:644
